TPU v7x, 32 devices: a whole 2x2x4 slice. The times are simulated.
32 devices in a mesh: grp: 4 (over x, core), sub: 8 (over z, y).
Axes of the slice: x: 2, y: 2, z: 4, core: 2. Of those that a mesh axis runs over, the one named last changes fastest.
Arguments:
- right_side: float32 [65536, 128], P(('grp', 'sub')), may hold values from -6 to 6
- fine_values: float32 [81, 65536], P(None, ('grp', 'sub')), as said below
- columns: int32 [81, 65536], P(None, ('grp', 'sub')), may hold values from 0 to 2175, as said below
- agg_map: int32 [65536], P(('grp', 'sub')), may hold values from 0 to 127
- send_lo: int32 [2048], P(('grp', 'sub')), may hold values from 0 to 2047
- send_hi: int32 [2048], P(('grp', 'sub')), may hold values from 0 to 2047
- coarse_matrix: float32 [4, 1024, 1024], P('grp', 'sub'), as said below
Outputs:
- solution: float32 [65536, 128], P(('grp', 'sub'))
- residual: float32 [65536, 128], P(('grp', 'sub'))
Inputs may be any that keep to these rules, and one draw needn't show every extreme that they name: `columns`: entry 0 of row i of a partition is 64 + i, the others lie within 64 positions of it. `fine_values`: entry 0 lies in 2.5 to 5 and every other entry's magnitude is at most 0.06. `coarse_matrix`: symmetric; the diagonal lies in 10 to 20, other entries' magnitudes are at most 7.1 / sqrt(1024).
All inputs are finite; a program needn't handle non-finite values.
Results may differ from a plain program's by a relative error of at most 0.0001.
Values sent between devices are 32-bit elements; how exact they have to be, the bound alone decides.
A program may use at most 128 MiB of HBM per device.

v0:
```python
import jax
import jax.numpy as jnp
from jax import lax
from jax.sharding import PartitionSpec as P

CHEB_FINE = 2
CHEB_COARSE = 6
CYCLES = 2
THETA = 1.0
DELTA = 0.7
OMEGA = 0.6
highest = lax.Precision.HIGHEST


def from_behind(shard, axis, by):
    peers = lax.axis_size(axis)
    pairs = [(i, i + by) for i in range(peers) if 0 <= i + by < peers]
    return lax.ppermute(shard, axis, pairs)


def band_tiles(fine_values, columns, block_rows):
    rows_dev = columns.shape[1]
    rows = jnp.arange(rows_dev, dtype=jnp.int32)
    starts = rows // block_rows * block_rows
    local = columns - starts[None, :]
    places = jnp.arange(2 * block_rows, dtype=jnp.int32)[None, :]
    tiles = jnp.zeros((rows_dev, 2 * block_rows), jnp.float32)
    for entry in range(columns.shape[0]):
        tiles = tiles + jnp.where(local[entry][:, None] == places, fine_values[entry][:, None], 0.0)
    tiles = tiles.reshape(rows_dev // block_rows, block_rows, 2 * block_rows)
    return (tiles[:, :, :block_rows], tiles[:, :, block_rows:])


def selector(indices, count):
    return (indices[:, None] == jnp.arange(count, dtype=jnp.int32)[None, :]).astype(jnp.float32)


def fine_apply(vector, low_tiles, high_tiles, pick_lo, pick_hi):
    upper_rows = jnp.dot(pick_hi, vector, precision=highest)
    lower_rows = jnp.dot(pick_lo, vector, precision=highest)
    below = from_behind(upper_rows, ("grp", "sub"), 1)
    above = from_behind(lower_rows, ("grp", "sub"), -1)
    extended = jnp.concatenate([below, vector, above], 0)
    block_rows = low_tiles.shape[1]
    pieces = extended.reshape(-1, block_rows, vector.shape[1])
    total = jnp.einsum("brc,bcn->brn", low_tiles, pieces[:-1], precision=highest)
    total = total + jnp.einsum("brc,bcn->brn", high_tiles, pieces[1:], precision=highest)
    return total.reshape(vector.shape)


def chebyshev(residual, apply, inverse, steps, final):
    rho_old = DELTA / THETA
    direction = inverse * residual / THETA
    result = direction
    for turn in range(1, steps):
        residual = residual - apply(direction)
        rho_new = 1.0 / (2.0 * THETA / DELTA - rho_old)
        direction = rho_new * rho_old * direction + 2.0 * rho_new / DELTA * inverse * residual
        result = result + direction
        rho_old = rho_new
    if final:
        residual = residual - apply(direction)
    return (result, residual)


def body(right_side, fine_values, columns, agg_map, send_lo, send_hi, coarse_matrix):
    rows_dev = right_side.shape[0]
    low_tiles, high_tiles = band_tiles(fine_values, columns, 2 * send_lo.shape[0])
    pick_lo = selector(send_lo, rows_dev)
    pick_hi = selector(send_hi, rows_dev)

    def apply_fine(vector):
        return fine_apply(vector, low_tiles, high_tiles, pick_lo, pick_hi)

    own_rows = coarse_matrix[0]
    aggregates = own_rows.shape[0]
    sub_index = lax.axis_index("sub")
    start = sub_index * aggregates
    block = lax.dynamic_slice_in_dim(own_rows, start, aggregates, 1)
    coarse_inverse = 1.0 / jnp.diagonal(block)[:, None]

    def apply_coarse(vector):
        whole = lax.all_gather(vector, "sub", axis=0, tiled=True)
        return jnp.dot(own_rows, whole, precision=highest)

    dinv = 1.0 / fine_values[0][:, None]
    onehot = selector(agg_map, aggregates)
    solution = jnp.zeros_like(right_side)
    residual = right_side
    for cycle in range(CYCLES):
        update, residual = chebyshev(residual, apply_fine, dinv, CHEB_FINE, True)
        solution = solution + update
        smoothed = residual - OMEGA * apply_fine(dinv * residual)
        coarse_rhs = jnp.einsum("ra,rn->an", onehot, smoothed, precision=highest)
        result, unused = chebyshev(coarse_rhs, apply_coarse, coarse_inverse, CHEB_COARSE, False)
        spread = jnp.dot(onehot, result, precision=highest)
        correction = spread - OMEGA * dinv * apply_fine(spread)
        solution = solution + correction
        residual = residual - apply_fine(correction)
        update, residual = chebyshev(residual, apply_fine, dinv, CHEB_FINE, True)
        solution = solution + update
    return (solution, residual)


def solution(mesh):
    placed = (
        P(("grp", "sub"), None),
        P(None, ("grp", "sub")),
        P(None, ("grp", "sub")),
        P(("grp", "sub")),
        P(("grp", "sub")),
        P(("grp", "sub")),
        P("grp", "sub", None),
    )
    return jax.shard_map(
        body,
        mesh=mesh,
        in_specs=placed,
        out_specs=(P(("grp", "sub"), None), P(("grp", "sub"), None)),
        check_vma=False,
    )
```

profile of v0, /device:TPU:29, one launch (start us, length us, event | category | flops | bytes accessed | tf_op | source)
XLA Modules:
  0.0 596.2 jit_solution(620123093191027239)
XLA Ops:
  9.6 7.1 %collective-permute-start = (f32[64,128]{1,0:T(8,128)}, f32[64,128]{1,0:T(8,128)S(1)}, u32[]{:S(2)}, u32[]{:S(2)}) collective-permute-start(f32[64,128]{1,0:T(8,128)} %fusion.65), channel_id=1, source_target_pairs={{0,1},{1,2},{2,3},{3,4},{4,5},{5,6},{6,7},{7,8},{8,9},{9,10},{10,1... | collective-permute-start | bytes 98312 | tf_op jit(solution)/shard_map/ppermute | solution.py:18
  21.6 47.7 %select_add_fusion = f32[16,128,256]{2,1,0:T(8,128)S(1)} fusion(f32[16,128]{1,0:T(8,128)S(1)} %bitcast.486, s32[16,128]{1,0:T(8,128)} %bitcast.608, f32[16,128]{1,0:T(8,128)S(1)} %bitcast.487, s32[16,128]{1,0:T(8,128)} %bitcast.609, f32[16,128]{1,0:T(8,128)S(1)} %bitcast.465, s32[16,128]{1,0:T(8,128)} %bitcast.610, f32[16,128]{1,0:T(8,128)S(1)} %bitcast.466, ...), kind=kLoop, calls=%fused_computation.1 | loop fusion | flops 126877696 | bytes 3424256 | tf_op jit(solution)/shard_map/add | solution.py:29
  82.1 5.4 collective-permute-done.3
  93.6 3.6 collective-permute-start.5
  97.2 5.2 collective-permute-done.5
  107.1 26.0 %all_gather.30 = f32[1024,128]{1,0:T(8,128)S(1)} all-gather(f32[128,128]{1,0:T(8,128)S(1)} %get-tuple-element.209), channel_id=1, replica_groups=mesh['grp'=4,'sub'=8] {'sub'}, dimensions={0}, use_global_device_ids=true | all-gather | bytes 589824 | tf_op jit(solution)/shard_map/all_gather | solution.py:83
  133.8 25.7 %all_gather.31 = f32[1024,128]{1,0:T(8,128)S(1)} all-gather(f32[128,128]{1,0:T(8,128)S(1)} %get-tuple-element.211), channel_id=1, replica_groups=mesh['grp'=4,'sub'=8] {'sub'}, dimensions={0}, use_global_device_ids=true | all-gather | bytes 589824 | tf_op jit(solution)/shard_map/all_gather | solution.py:83
  160.1 25.7 %all_gather.32 = f32[1024,128]{1,0:T(8,128)S(1)} all-gather(f32[128,128]{1,0:T(8,128)S(1)} %get-tuple-element.213), channel_id=1, replica_groups=mesh['grp'=4,'sub'=8] {'sub'}, dimensions={0}, use_global_device_ids=true | all-gather | bytes 589824 | tf_op jit(solution)/shard_map/all_gather | solution.py:83
  186.5 25.4 %all_gather.33 = f32[1024,128]{1,0:T(8,128)S(1)} all-gather(f32[128,128]{1,0:T(8,128)S(1)} %get-tuple-element.215), channel_id=1, replica_groups=mesh['grp'=4,'sub'=8] {'sub'}, dimensions={0}, use_global_device_ids=true | all-gather | bytes 589824 | tf_op jit(solution)/shard_map/all_gather | solution.py:83
  212.5 25.6 %all_gather.34 = f32[1024,128]{1,0:T(8,128)S(1)} all-gather(f32[128,128]{1,0:T(8,128)S(1)} %get-tuple-element.217), channel_id=1, replica_groups=mesh['grp'=4,'sub'=8] {'sub'}, dimensions={0}, use_global_device_ids=true | all-gather | bytes 589824 | tf_op jit(solution)/shard_map/all_gather | solution.py:83
  240.8 30.2 %collective-permute-start.6 = (f32[64,128]{1,0:T(8,128)S(1)}, f32[64,128]{1,0:T(8,128)S(1)}, u32[]{:S(2)}, u32[]{:S(2)}) collective-permute-start(f32[64,128]{1,0:T(8,128)S(1)} %fusion.62), channel_id=1, source_target_pairs={{0,1},{1,2},{2,3},{3,4},{4,5},{5,6},{6,7},{7,8},{8,9},{9,10},{10,1... | collective-permute-start | bytes 98312 | tf_op jit(solution)/shard_map/ppermute | solution.py:18
  273.2 6.6 %collective-permute-done.7 = f32[64,128]{1,0:T(8,128)S(1)} collective-permute-done((f32[64,128]{1,0:T(8,128)S(1)}, f32[64,128]{1,0:T(8,128)S(1)}, u32[]{:S(2)}, u32[]{:S(2)}) %collective-permute-start.7) | collective-permute-done | bytes 32800 | tf_op jit(solution)/shard_map/ppermute | solution.py:18
  289.3 5.4 collective-permute-done.9
  300.7 3.8 collective-permute-start.11
  304.5 5.0 collective-permute-done.11
  318.9 5.4 collective-permute-done.13
  330.3 3.5 collective-permute-start.15
  333.9 5.3 collective-permute-done.15
  348.6 5.4 collective-permute-done.17
  360.0 3.6 collective-permute-start.19
  363.6 5.2 collective-permute-done.19
  373.0 24.9 %all_gather.35 = f32[1024,128]{1,0:T(8,128)S(1)} all-gather(f32[128,128]{1,0:T(8,128)S(1)} %get-tuple-element.219), channel_id=1, replica_groups=mesh['grp'=4,'sub'=8] {'sub'}, dimensions={0}, use_global_device_ids=true | all-gather | bytes 589824 | tf_op jit(solution)/shard_map/all_gather | solution.py:83
  398.5 25.4 %all_gather.36 = f32[1024,128]{1,0:T(8,128)S(1)} all-gather(f32[128,128]{1,0:T(8,128)S(1)} %get-tuple-element.221), channel_id=1, replica_groups=mesh['grp'=4,'sub'=8] {'sub'}, dimensions={0}, use_global_device_ids=true | all-gather | bytes 589824 | tf_op jit(solution)/shard_map/all_gather | solution.py:83
  424.6 26.1 %all_gather.37 = f32[1024,128]{1,0:T(8,128)S(1)} all-gather(f32[128,128]{1,0:T(8,128)S(1)} %get-tuple-element.223), channel_id=1, replica_groups=mesh['grp'=4,'sub'=8] {'sub'}, dimensions={0}, use_global_device_ids=true | all-gather | bytes 589824 | tf_op jit(solution)/shard_map/all_gather | solution.py:83
  451.3 25.9 %all_gather.38 = f32[1024,128]{1,0:T(8,128)S(1)} all-gather(f32[128,128]{1,0:T(8,128)S(1)} %get-tuple-element.225), channel_id=1, replica_groups=mesh['grp'=4,'sub'=8] {'sub'}, dimensions={0}, use_global_device_ids=true | all-gather | bytes 589824 | tf_op jit(solution)/shard_map/all_gather | solution.py:83
  477.8 25.3 %all_gather.39 = f32[1024,128]{1,0:T(8,128)S(1)} all-gather(f32[128,128]{1,0:T(8,128)S(1)} %get-tuple-element.227), channel_id=1, replica_groups=mesh['grp'=4,'sub'=8] {'sub'}, dimensions={0}, use_global_device_ids=true | all-gather | bytes 589824 | tf_op jit(solution)/shard_map/all_gather | solution.py:83
  505.8 31.2 %collective-permute-start.20 = (f32[64,128]{1,0:T(8,128)S(1)}, f32[64,128]{1,0:T(8,128)S(1)}, u32[]{:S(2)}, u32[]{:S(2)}) collective-permute-start(f32[64,128]{1,0:T(8,128)S(1)} %fusion.55), channel_id=1, source_target_pairs={{0,1},{1,2},{2,3},{3,4},{4,5},{5,6},{6,7},{7,8},{8,9},{9,10},{10,1... | collective-permute-start | bytes 98312 | tf_op jit(solution)/shard_map/ppermute | solution.py:18
  539.3 6.6 %collective-permute-done.21 = f32[64,128]{1,0:T(8,128)S(1)} collective-permute-done((f32[64,128]{1,0:T(8,128)S(1)}, f32[64,128]{1,0:T(8,128)S(1)}, u32[]{:S(2)}, u32[]{:S(2)}) %collective-permute-start.21) | collective-permute-done | bytes 32800 | tf_op jit(solution)/shard_map/ppermute | solution.py:18
  555.3 5.6 collective-permute-done.23
  566.9 3.7 collective-permute-start.25
  570.5 5.2 collective-permute-done.25
  586.5 5.4 collective-permute-done.27
  (168 shorter events, 131.6 us)
Async XLA Ops:
  0.6 21.0 %copy-start = (f32[1,128,1024]{2,1,0:T(8,128)S(1)}, f32[1,128,1024]{2,1,0:T(8,128)}, u32[]{:S(2)}) copy-start(f32[1,128,1024]{2,1,0:T(8,128)} %param.13) | copy-start | bytes 1572868
  0.6 16.1 %copy-start.4 = (f32[81,2048]{1,0:T(8,128)S(1)}, f32[81,2048]{1,0:T(8,128)}, u32[]{:S(2)}) copy-start(f32[81,2048]{1,0:T(8,128)} %param.8) | copy-start | bytes 1990660
  0.7 16.5 %copy-start.3 = (s32[81,2048]{1,0:T(8,128)S(1)}, s32[81,2048]{1,0:T(8,128)}, u32[]{:S(2)}) copy-start(s32[81,2048]{1,0:T(8,128)} %param.9) | copy-start | bytes 1990660
  4.9 65.7 %collective-permute-start.1 = (f32[64,128]{1,0:T(8,128)}, f32[64,128]{1,0:T(8,128)S(1)}, u32[]{:S(2)}, u32[]{:S(2)}) collective-permute-start(f32[64,128]{1,0:T(8,128)} %fusion.51), channel_id=1, source_target_pairs={{1,0},{2,1},{3,2},{4,3},{5,4},{6,5},{7,6},{8,7},{9,8},{10,9},{11,1... | collective-permute-start | bytes 98312 | tf_op jit(solution)/shard_map/ppermute | solution.py:18
  9.6 10.7 %copy-start.1 = (f32[2048,128]{1,0:T(8,128)S(1)}, f32[2048,128]{1,0:T(8,128)}, u32[]{:S(2)}) copy-start(f32[2048,128]{1,0:T(8,128)} %param.7) | copy-start | bytes 3145732
  9.6 61.1 %collective-permute-start = (f32[64,128]{1,0:T(8,128)}, f32[64,128]{1,0:T(8,128)S(1)}, u32[]{:S(2)}, u32[]{:S(2)}) collective-permute-start(f32[64,128]{1,0:T(8,128)} %fusion.65), channel_id=1, source_target_pairs={{0,1},{1,2},{2,3},{3,4},{4,5},{5,6},{6,7},{7,8},{8,9},{9,10},{10,1... | collective-permute-start | bytes 98312 | tf_op jit(solution)/shard_map/ppermute | solution.py:18
  76.7 5.3 collective-permute-start.2
  78.7 8.8 %collective-permute-start.3 = (f32[64,128]{1,0:T(8,128)S(1)}, f32[64,128]{1,0:T(8,128)S(1)}, u32[]{:S(2)}, u32[]{:S(2)}) collective-permute-start(f32[64,128]{1,0:T(8,128)S(1)} %fusion.50), channel_id=1, source_target_pairs={{1,0},{2,1},{3,2},{4,3},{5,4},{6,5},{7,6},{8,7},{9,8},{10,9},{11,1... | collective-permute-start | bytes 98312 | tf_op jit(solution)/shard_map/ppermute | solution.py:18
  91.7 5.5 collective-permute-start.4
  93.6 8.8 %collective-permute-start.5 = (f32[64,128]{1,0:T(8,128)S(1)}, f32[64,128]{1,0:T(8,128)S(1)}, u32[]{:S(2)}, u32[]{:S(2)}) collective-permute-start(f32[64,128]{1,0:T(8,128)S(1)} %fusion.49), channel_id=1, source_target_pairs={{1,0},{2,1},{3,2},{4,3},{5,4},{6,5},{7,6},{8,7},{9,8},{10,9},{11,1... | collective-permute-start | bytes 98312 | tf_op jit(solution)/shard_map/ppermute | solution.py:18
  240.8 32.4 %collective-permute-start.6 = (f32[64,128]{1,0:T(8,128)S(1)}, f32[64,128]{1,0:T(8,128)S(1)}, u32[]{:S(2)}, u32[]{:S(2)}) collective-permute-start(f32[64,128]{1,0:T(8,128)S(1)} %fusion.62), channel_id=1, source_target_pairs={{0,1},{1,2},{2,3},{3,4},{4,5},{5,6},{6,7},{7,8},{8,9},{9,10},{10,1... | collective-permute-start | bytes 98312 | tf_op jit(solution)/shard_map/ppermute | solution.py:18
  271.0 8.8 %collective-permute-start.7 = (f32[64,128]{1,0:T(8,128)S(1)}, f32[64,128]{1,0:T(8,128)S(1)}, u32[]{:S(2)}, u32[]{:S(2)}) collective-permute-start(f32[64,128]{1,0:T(8,128)S(1)} %fusion.48), channel_id=1, source_target_pairs={{1,0},{2,1},{3,2},{4,3},{5,4},{6,5},{7,6},{8,7},{9,8},{10,9},{11,1... | collective-permute-start | bytes 98312 | tf_op jit(solution)/shard_map/ppermute | solution.py:18
  284.0 5.3 collective-permute-start.8
  285.9 8.8 %collective-permute-start.9 = (f32[64,128]{1,0:T(8,128)S(1)}, f32[64,128]{1,0:T(8,128)S(1)}, u32[]{:S(2)}, u32[]{:S(2)}) collective-permute-start(f32[64,128]{1,0:T(8,128)S(1)} %fusion.47), channel_id=1, source_target_pairs={{1,0},{2,1},{3,2},{4,3},{5,4},{6,5},{7,6},{8,7},{9,8},{10,9},{11,1... | collective-permute-start | bytes 98312 | tf_op jit(solution)/shard_map/ppermute | solution.py:18
  298.8 5.8 collective-permute-start.10
  300.7 8.8 %collective-permute-start.11 = (f32[64,128]{1,0:T(8,128)S(1)}, f32[64,128]{1,0:T(8,128)S(1)}, u32[]{:S(2)}, u32[]{:S(2)}) collective-permute-start(f32[64,128]{1,0:T(8,128)S(1)} %fusion.46), channel_id=1, source_target_pairs={{1,0},{2,1},{3,2},{4,3},{5,4},{6,5},{7,6},{8,7},{9,8},{10,9},{11,1... | collective-permute-start | bytes 98312 | tf_op jit(solution)/shard_map/ppermute | solution.py:18
  313.6 5.3 collective-permute-start.12
  315.5 8.8 %collective-permute-start.13 = (f32[64,128]{1,0:T(8,128)S(1)}, f32[64,128]{1,0:T(8,128)S(1)}, u32[]{:S(2)}, u32[]{:S(2)}) collective-permute-start(f32[64,128]{1,0:T(8,128)S(1)} %fusion.45), channel_id=1, source_target_pairs={{1,0},{2,1},{3,2},{4,3},{5,4},{6,5},{7,6},{8,7},{9,8},{10,9},{11,1... | collective-permute-start | bytes 98312 | tf_op jit(solution)/shard_map/ppermute | solution.py:18
  328.4 5.5 collective-permute-start.14
  330.3 8.8 %collective-permute-start.15 = (f32[64,128]{1,0:T(8,128)S(1)}, f32[64,128]{1,0:T(8,128)S(1)}, u32[]{:S(2)}, u32[]{:S(2)}) collective-permute-start(f32[64,128]{1,0:T(8,128)S(1)} %fusion.44), channel_id=1, source_target_pairs={{1,0},{2,1},{3,2},{4,3},{5,4},{6,5},{7,6},{8,7},{9,8},{10,9},{11,1... | collective-permute-start | bytes 98312 | tf_op jit(solution)/shard_map/ppermute | solution.py:18
  343.2 5.3 collective-permute-start.16
  345.2 8.8 %collective-permute-start.17 = (f32[64,128]{1,0:T(8,128)S(1)}, f32[64,128]{1,0:T(8,128)S(1)}, u32[]{:S(2)}, u32[]{:S(2)}) collective-permute-start(f32[64,128]{1,0:T(8,128)S(1)} %fusion.43), channel_id=1, source_target_pairs={{1,0},{2,1},{3,2},{4,3},{5,4},{6,5},{7,6},{8,7},{9,8},{10,9},{11,1... | collective-permute-start | bytes 98312 | tf_op jit(solution)/shard_map/ppermute | solution.py:18
  358.1 5.5 collective-permute-start.18
  360.0 8.8 %collective-permute-start.19 = (f32[64,128]{1,0:T(8,128)S(1)}, f32[64,128]{1,0:T(8,128)S(1)}, u32[]{:S(2)}, u32[]{:S(2)}) collective-permute-start(f32[64,128]{1,0:T(8,128)S(1)} %fusion.42), channel_id=1, source_target_pairs={{1,0},{2,1},{3,2},{4,3},{5,4},{6,5},{7,6},{8,7},{9,8},{10,9},{11,1... | collective-permute-start | bytes 98312 | tf_op jit(solution)/shard_map/ppermute | solution.py:18
  505.8 33.4 %collective-permute-start.20 = (f32[64,128]{1,0:T(8,128)S(1)}, f32[64,128]{1,0:T(8,128)S(1)}, u32[]{:S(2)}, u32[]{:S(2)}) collective-permute-start(f32[64,128]{1,0:T(8,128)S(1)} %fusion.55), channel_id=1, source_target_pairs={{0,1},{1,2},{2,3},{3,4},{4,5},{5,6},{6,7},{7,8},{8,9},{9,10},{10,1... | collective-permute-start | bytes 98312 | tf_op jit(solution)/shard_map/ppermute | solution.py:18
  537.1 8.8 %collective-permute-start.21 = (f32[64,128]{1,0:T(8,128)S(1)}, f32[64,128]{1,0:T(8,128)S(1)}, u32[]{:S(2)}, u32[]{:S(2)}) collective-permute-start(f32[64,128]{1,0:T(8,128)S(1)} %fusion.41), channel_id=1, source_target_pairs={{1,0},{2,1},{3,2},{4,3},{5,4},{6,5},{7,6},{8,7},{9,8},{10,9},{11,1... | collective-permute-start | bytes 98312 | tf_op jit(solution)/shard_map/ppermute | solution.py:18
  550.0 5.3 collective-permute-start.22
  551.9 8.9 %collective-permute-start.23 = (f32[64,128]{1,0:T(8,128)S(1)}, f32[64,128]{1,0:T(8,128)S(1)}, u32[]{:S(2)}, u32[]{:S(2)}) collective-permute-start(f32[64,128]{1,0:T(8,128)S(1)} %fusion.40), channel_id=1, source_target_pairs={{1,0},{2,1},{3,2},{4,3},{5,4},{6,5},{7,6},{8,7},{9,8},{10,9},{11,1... | collective-permute-start | bytes 98312 | tf_op jit(solution)/shard_map/ppermute | solution.py:18
  564.9 5.6 collective-permute-start.24
  566.9 8.8 %collective-permute-start.25 = (f32[64,128]{1,0:T(8,128)S(1)}, f32[64,128]{1,0:T(8,128)S(1)}, u32[]{:S(2)}, u32[]{:S(2)}) collective-permute-start(f32[64,128]{1,0:T(8,128)S(1)} %fusion.39), channel_id=1, source_target_pairs={{1,0},{2,1},{3,2},{4,3},{5,4},{6,5},{7,6},{8,7},{9,8},{10,9},{11,1... | collective-permute-start | bytes 98312 | tf_op jit(solution)/shard_map/ppermute | solution.py:18
  581.2 5.3 collective-permute-start.26
  583.1 8.8 %collective-permute-start.27 = (f32[64,128]{1,0:T(8,128)S(1)}, f32[64,128]{1,0:T(8,128)S(1)}, u32[]{:S(2)}, u32[]{:S(2)}) collective-permute-start(f32[64,128]{1,0:T(8,128)S(1)} %fusion.38), channel_id=1, source_target_pairs={{1,0},{2,1},{3,2},{4,3},{5,4},{6,5},{7,6},{8,7},{9,8},{10,9},{11,1... | collective-permute-start | bytes 98312 | tf_op jit(solution)/shard_map/ppermute | solution.py:18
  (4 other events, 4.2 us)
where the time goes:
time: 600 us; the launch traced here: 596 us
  blocking collectives  256 us (43%)
  starting transfers between devices  135 us (22%)
  waiting for transfers between devices  72 us (12%)
  matrix products  64.9 us (11%)
  other arithmetic  61.3 us (10%)
    all_gather x10, blocking collectives, apply_coarse(): whole = lax.all_gather(vector, 'sub', axis=0, tiled=True)  256 us
    ppermute x28, starting transfers between devices, from_behind(): return lax.ppermute(shard, axis, pairs)  135 us
    ppermute x28, waiting for transfers between devices, from_behind(): return lax.ppermute(shard, axis, pairs)  72 us
    add x1, other arithmetic, band_tiles(): tiles + jnp.where(local[entry][:, None] == places, fine_values[entry][:,...  47.7 us
    dot_general x14, matrix products, fine_apply(): jnp.einsum('brc,bcn->brn', low_tiles, pieces[:-1], precision=highest)  17.3 us
    dot_general x14, matrix products, fine_apply(): jnp.einsum('brc,bcn->brn', high_tiles, pieces[1:], precision=highest)  16.8 us
  transfers between devices with their start and end apart: 28, of which 13 were waited for; matrix products, arithmetic and copies ran while one was open for 9% of the time, Pallas kernels for 0%

commit v1 on v0

--- a/solution.py
+++ b/solution.py
@@ -10,6 +10,26 @@
 DELTA = 0.7
 OMEGA = 0.6
 highest = lax.Precision.HIGHEST
+
+
+def lead_the_slot(x_part, axis_tag):
+    world_n = lax.axis_size(axis_tag)
+    new = range(world_n)
+    long_array = map(lambda dev: (dev, (dev + 1) % world_n), new)
+    all_blocks = list(long_array)
+    next_value = range(world_n)
+    current_arr = map(lambda dev: (dev, (dev - 1) % world_n), next_value)
+    table = list(current_arr)
+    newest, b_next = ([x_part], [x_part])
+    for _ in range(world_n // 2):
+        piece_now = lax.ppermute(newest[-1], axis_tag, all_blocks)
+        newest.append(piece_now)
+    for _ in range((world_n - 1) // 2):
+        res = lax.ppermute(b_next[-1], axis_tag, table)
+        b_next.append(res)
+    piece_out = jnp.concatenate([*newest[::-1], *b_next[1:]], axis=0)
+    y2 = lax.axis_index(axis_tag)
+    return jnp.roll(piece_out, (y2 - world_n // 2) * x_part.shape[0], axis=0)
 
 
 def from_behind(shard, axis, by):
@@ -80,7 +100,7 @@
     coarse_inverse = 1.0 / jnp.diagonal(block)[:, None]
 
     def apply_coarse(vector):
-        whole = lax.all_gather(vector, "sub", axis=0, tiled=True)
+        whole = lead_the_slot(vector, "sub")
         return jnp.dot(own_rows, whole, precision=highest)
 
     dinv = 1.0 / fine_values[0][:, None]

time: 600 us -> 572 us (0.953)
  blocking collectives: 256 us -> 0 us
  waiting for transfers between devices: 72 us -> 189 us
  starting transfers between devices: 135 us -> 240 us
    all_gather x10 -> x0, blocking collectives: 256 us -> none  [apply_coarse(): whole = lax.all_gather(vector, 'sub', axis=0, tiled=True)]
    ppermute x0 -> x70, starting transfers between devices: none -> 120 us  [the longest x40 120 us: lead_the_slot(): piece_now = lax.ppermute(newest[-1], axis_tag, all_blocks)]
    ppermute x0 -> x70, waiting for transfers between devices: none -> 118 us  [the longest x40 71.9 us: lead_the_slot(): piece_now = lax.ppermute(newest[-1], axis_tag, all_blocks)]
    ppermute x28, starting transfers between devices: 135 us -> 120 us  [from_behind(): return lax.ppermute(shard, axis, pairs)]
  transfers between devices with their start and end apart: 28 -> 98, of which waited for: 13 -> 69; matrix products, arithmetic and copies ran while one was open for 9% -> 10% of each run, Pallas kernels for 0% -> 0%
where the time goes in v1:
time: 572 us; the launch traced here: 568 us
  starting transfers between devices  240 us (42%)
  waiting for transfers between devices  189 us (33%)
  matrix products  66.9 us (12%)
  other arithmetic  61.8 us (11%)
  local copies, waits for them, and re-layouts  6.73 us (1%)
    ppermute x28, starting transfers between devices, from_behind(): return lax.ppermute(shard, axis, pairs)  120 us
    ppermute x40, starting transfers between devices, lead_the_slot(): piece_now = lax.ppermute(newest[-1], axis_tag, all_blocks)  120 us
    ppermute x40, waiting for transfers between devices, lead_the_slot(): piece_now = lax.ppermute(newest[-1], axis_tag, all_blocks)  71.9 us
    ppermute x28, waiting for transfers between devices, from_behind(): return lax.ppermute(shard, axis, pairs)  71 us
    add x1, other arithmetic, band_tiles(): tiles + jnp.where(local[entry][:, None] == places, fine_values[entry][:,...  46.7 us
    ppermute x30, waiting for transfers between devices, lead_the_slot(): res = lax.ppermute(b_next[-1], axis_tag, table)  46.4 us
    dot_general x14, matrix products, fine_apply(): jnp.einsum('brc,bcn->brn', low_tiles, pieces[:-1], precision=highest)  17.3 us
    dot_general x14, matrix products, fine_apply(): jnp.einsum('brc,bcn->brn', high_tiles, pieces[1:], precision=highest)  16.7 us
  transfers between devices with their start and end apart: 98, of which 69 were waited for; matrix products, arithmetic and copies ran while one was open for 10% of the time, Pallas kernels for 0%

profile of v1, /device:TPU:29, one launch (start us, length us, event | category | flops | bytes accessed | tf_op | source)
XLA Modules:
  0.0 567.9 jit_solution(3810402405419202775)
XLA Ops:
  9.5 7.1 %collective-permute-start = (f32[64,128]{1,0:T(8,128)}, f32[64,128]{1,0:T(8,128)S(1)}, u32[]{:S(2)}, u32[]{:S(2)}) collective-permute-start(f32[64,128]{1,0:T(8,128)} %fusion.85), channel_id=1, source_target_pairs={{0,1},{1,2},{2,3},{3,4},{4,5},{5,6},{6,7},{7,8},{8,9},{9,10},{10,1... | collective-permute-start | bytes 98312 | tf_op jit(solution)/shard_map/ppermute | solution.py:38
  21.5 46.7 %select_add_fusion = f32[16,128,256]{2,1,0:T(8,128)S(1)} fusion(f32[16,128]{1,0:T(8,128)S(1)} %bitcast.476, s32[16,128]{1,0:T(8,128)} %bitcast.598, f32[16,128]{1,0:T(8,128)S(1)} %bitcast.477, s32[16,128]{1,0:T(8,128)} %bitcast.599, f32[16,128]{1,0:T(8,128)S(1)} %bitcast.455, s32[16,128]{1,0:T(8,128)} %bitcast.600, f32[16,128]{1,0:T(8,128)S(1)} %bitcast.456, ...), kind=kLoop, calls=%fused_computation.1 | loop fusion | flops 126877696 | bytes 3424256 | tf_op jit(solution)/shard_map/add | solution.py:49
  97.2 5.0 collective-permute-done.5
  114.1 4.5 collective-permute-start.8
  119.9 5.0 collective-permute-start.9
  150.7 4.6 collective-permute-done.19
  169.2 4.6 collective-permute-start.23
  194.0 4.9 collective-permute-start.30
  212.9 4.6 collective-permute-start.36
  218.8 4.5 collective-permute-start.37
  224.7 4.6 collective-permute-done.40
  232.2 24.5 %collective-permute-start.41 = (f32[64,128]{1,0:T(8,128)S(1)}, f32[64,128]{1,0:T(8,128)S(1)}, u32[]{:S(2)}, u32[]{:S(2)}) collective-permute-start(f32[64,128]{1,0:T(8,128)S(1)} %fusion.82), channel_id=1, source_target_pairs={{0,1},{1,2},{2,3},{3,4},{4,5},{5,6},{6,7},{7,8},{8,9},{9,10},{10,1... | collective-permute-start | bytes 98312 | tf_op jit(solution)/shard_map/ppermute | solution.py:38
  258.7 6.9 %collective-permute-done.42 = f32[64,128]{1,0:T(8,128)S(1)} collective-permute-done((f32[64,128]{1,0:T(8,128)S(1)}, f32[64,128]{1,0:T(8,128)S(1)}, u32[]{:S(2)}, u32[]{:S(2)}) %collective-permute-start.42) | collective-permute-done | bytes 32800 | tf_op jit(solution)/shard_map/ppermute | solution.py:38
  274.9 5.4 collective-permute-done.44
  290.0 5.2 collective-permute-done.46
  304.6 5.4 collective-permute-done.48
  319.8 5.0 collective-permute-done.50
  334.2 5.4 collective-permute-done.52
  349.3 5.3 collective-permute-done.54
  366.4 4.7 collective-permute-start.57
  378.3 4.5 collective-permute-done.61
  402.9 5.2 collective-permute-done.68
  416.6 4.5 collective-permute-start.71
  422.4 4.6 collective-permute-start.72
  441.0 4.5 collective-permute-start.78
  447.3 4.9 collective-permute-start.79
  478.0 4.6 collective-permute-done.89
  485.6 23.3 %collective-permute-start.90 = (f32[64,128]{1,0:T(8,128)S(1)}, f32[64,128]{1,0:T(8,128)S(1)}, u32[]{:S(2)}, u32[]{:S(2)}) collective-permute-start(f32[64,128]{1,0:T(8,128)S(1)} %fusion.75), channel_id=1, source_target_pairs={{0,1},{1,2},{2,3},{3,4},{4,5},{5,6},{6,7},{7,8},{8,9},{9,10},{10,1... | collective-permute-start | bytes 98312 | tf_op jit(solution)/shard_map/ppermute | solution.py:38
  510.8 6.9 %collective-permute-done.91 = f32[64,128]{1,0:T(8,128)S(1)} collective-permute-done((f32[64,128]{1,0:T(8,128)S(1)}, f32[64,128]{1,0:T(8,128)S(1)}, u32[]{:S(2)}, u32[]{:S(2)}) %collective-permute-start.91) | collective-permute-done | bytes 32800 | tf_op jit(solution)/shard_map/ppermute | solution.py:38
  527.0 5.4 collective-permute-done.93
  542.1 5.2 collective-permute-done.95
  558.4 5.4 collective-permute-done.97
  (394 shorter events, 322.0 us)
Async XLA Ops:
  4.9 63.4 %collective-permute-start.1 = (f32[64,128]{1,0:T(8,128)}, f32[64,128]{1,0:T(8,128)S(1)}, u32[]{:S(2)}, u32[]{:S(2)}) collective-permute-start(f32[64,128]{1,0:T(8,128)} %fusion.71), channel_id=1, source_target_pairs={{1,0},{2,1},{3,2},{4,3},{5,4},{6,5},{7,6},{8,7},{9,8},{10,9},{11,1... | collective-permute-start | bytes 98312 | tf_op jit(solution)/shard_map/ppermute | solution.py:38
  9.5 58.8 %collective-permute-start = (f32[64,128]{1,0:T(8,128)}, f32[64,128]{1,0:T(8,128)S(1)}, u32[]{:S(2)}, u32[]{:S(2)}) collective-permute-start(f32[64,128]{1,0:T(8,128)} %fusion.85), channel_id=1, source_target_pairs={{0,1},{1,2},{2,3},{3,4},{4,5},{5,6},{6,7},{7,8},{8,9},{9,10},{10,1... | collective-permute-start | bytes 98312 | tf_op jit(solution)/shard_map/ppermute | solution.py:38
  74.8 6.6 %collective-permute-start.2 = (f32[64,128]{1,0:T(8,128)S(1)}, f32[64,128]{1,0:T(8,128)S(1)}, u32[]{:S(2)}, u32[]{:S(2)}) collective-permute-start(f32[64,128]{1,0:T(8,128)S(1)} %fusion.84), channel_id=1, source_target_pairs={{0,1},{1,2},{2,3},{3,4},{4,5},{5,6},{6,7},{7,8},{8,9},{9,10},{10,1... | collective-permute-start | bytes 98312 | tf_op jit(solution)/shard_map/ppermute | solution.py:38
  76.8 8.8 %collective-permute-start.3 = (f32[64,128]{1,0:T(8,128)S(1)}, f32[64,128]{1,0:T(8,128)S(1)}, u32[]{:S(2)}, u32[]{:S(2)}) collective-permute-start(f32[64,128]{1,0:T(8,128)S(1)} %fusion.70), channel_id=1, source_target_pairs={{1,0},{2,1},{3,2},{4,3},{5,4},{6,5},{7,6},{8,7},{9,8},{10,9},{11,1... | collective-permute-start | bytes 98312 | tf_op jit(solution)/shard_map/ppermute | solution.py:38
  93.4 8.8 %collective-permute-start.5 = (f32[64,128]{1,0:T(8,128)S(1)}, f32[64,128]{1,0:T(8,128)S(1)}, u32[]{:S(2)}, u32[]{:S(2)}) collective-permute-start(f32[64,128]{1,0:T(8,128)S(1)} %fusion.69), channel_id=1, source_target_pairs={{1,0},{2,1},{3,2},{4,3},{5,4},{6,5},{7,6},{8,7},{9,8},{10,9},{11,1... | collective-permute-start | bytes 98312 | tf_op jit(solution)/shard_map/ppermute | solution.py:38
  112.8 6.2 %collective-permute-start.10 = (f32[128,128]{1,0:T(8,128)S(1)}, f32[128,128]{1,0:T(8,128)S(1)}, u32[]{:S(2)}, u32[]{:S(2)}) collective-permute-start(f32[128,128]{1,0:T(8,128)S(1)} %get-tuple-element.210), channel_id=1, source_target_pairs={{0,7},{1,0},{2,1},{3,2},{4,3},{5,4},{6,5},{7,6},{8,15},{9,8},{10,9... | collective-permute-start | bytes 196616 | tf_op jit(solution)/shard_map/ppermute | solution.py:28
  119.0 6.0 %collective-permute-start.11 = (f32[128,128]{1,0:T(8,128)S(1)}, f32[128,128]{1,0:T(8,128)S(1)}, u32[]{:S(2)}, u32[]{:S(2)}) collective-permute-start(f32[128,128]{1,0:T(8,128)S(1)} %collective-permute-done.10), channel_id=1, source_target_pairs={{0,7},{1,0},{2,1},{3,2},{4,3},{5,4},{6,5},{7,6},{8,15},{9,8},{10,9... | collective-permute-start | bytes 196616 | tf_op jit(solution)/shard_map/ppermute | solution.py:28
  119.9 6.4 %collective-permute-start.9 = (f32[128,128]{1,0:T(8,128)S(1)}, f32[128,128]{1,0:T(8,128)S(1)}, u32[]{:S(2)}, u32[]{:S(2)}) collective-permute-start(f32[128,128]{1,0:T(8,128)S(1)} %collective-permute-done.8), channel_id=1, source_target_pairs={{0,1},{1,2},{2,3},{3,4},{4,5},{5,6},{6,7},{7,0},{8,9},{9,10},{10,1... | collective-permute-start | bytes 196616 | tf_op jit(solution)/shard_map/ppermute | solution.py:25
  187.8 6.2 %collective-permute-start.29 = (f32[128,128]{1,0:T(8,128)S(1)}, f32[128,128]{1,0:T(8,128)S(1)}, u32[]{:S(2)}, u32[]{:S(2)}) collective-permute-start(f32[128,128]{1,0:T(8,128)S(1)} %collective-permute-done.28), channel_id=1, source_target_pairs={{0,1},{1,2},{2,3},{3,4},{4,5},{5,6},{6,7},{7,0},{8,9},{9,10},{10,1... | collective-permute-start | bytes 196616 | tf_op jit(solution)/shard_map/ppermute | solution.py:25
  192.3 6.6 %collective-permute-start.32 = (f32[128,128]{1,0:T(8,128)S(1)}, f32[128,128]{1,0:T(8,128)S(1)}, u32[]{:S(2)}, u32[]{:S(2)}) collective-permute-start(f32[128,128]{1,0:T(8,128)S(1)} %collective-permute-done.31), channel_id=1, source_target_pairs={{0,7},{1,0},{2,1},{3,2},{4,3},{5,4},{6,5},{7,6},{8,15},{9,8},{10,9... | collective-permute-start | bytes 196616 | tf_op jit(solution)/shard_map/ppermute | solution.py:28
  194.0 6.2 %collective-permute-start.30 = (f32[128,128]{1,0:T(8,128)S(1)}, f32[128,128]{1,0:T(8,128)S(1)}, u32[]{:S(2)}, u32[]{:S(2)}) collective-permute-start(f32[128,128]{1,0:T(8,128)S(1)} %collective-permute-done.29), channel_id=1, source_target_pairs={{0,1},{1,2},{2,3},{3,4},{4,5},{5,6},{6,7},{7,0},{8,9},{9,10},{10,1... | collective-permute-start | bytes 196616 | tf_op jit(solution)/shard_map/ppermute | solution.py:25
  232.2 26.5 %collective-permute-start.41 = (f32[64,128]{1,0:T(8,128)S(1)}, f32[64,128]{1,0:T(8,128)S(1)}, u32[]{:S(2)}, u32[]{:S(2)}) collective-permute-start(f32[64,128]{1,0:T(8,128)S(1)} %fusion.82), channel_id=1, source_target_pairs={{0,1},{1,2},{2,3},{3,4},{4,5},{5,6},{6,7},{7,8},{8,9},{9,10},{10,1... | collective-permute-start | bytes 98312 | tf_op jit(solution)/shard_map/ppermute | solution.py:38
  256.8 8.8 %collective-permute-start.42 = (f32[64,128]{1,0:T(8,128)S(1)}, f32[64,128]{1,0:T(8,128)S(1)}, u32[]{:S(2)}, u32[]{:S(2)}) collective-permute-start(f32[64,128]{1,0:T(8,128)S(1)} %fusion.68), channel_id=1, source_target_pairs={{1,0},{2,1},{3,2},{4,3},{5,4},{6,5},{7,6},{8,7},{9,8},{10,9},{11,1... | collective-permute-start | bytes 98312 | tf_op jit(solution)/shard_map/ppermute | solution.py:38
  271.6 8.8 %collective-permute-start.44 = (f32[64,128]{1,0:T(8,128)S(1)}, f32[64,128]{1,0:T(8,128)S(1)}, u32[]{:S(2)}, u32[]{:S(2)}) collective-permute-start(f32[64,128]{1,0:T(8,128)S(1)} %fusion.67), channel_id=1, source_target_pairs={{1,0},{2,1},{3,2},{4,3},{5,4},{6,5},{7,6},{8,7},{9,8},{10,9},{11,1... | collective-permute-start | bytes 98312 | tf_op jit(solution)/shard_map/ppermute | solution.py:38
  286.4 8.8 %collective-permute-start.46 = (f32[64,128]{1,0:T(8,128)S(1)}, f32[64,128]{1,0:T(8,128)S(1)}, u32[]{:S(2)}, u32[]{:S(2)}) collective-permute-start(f32[64,128]{1,0:T(8,128)S(1)} %fusion.66), channel_id=1, source_target_pairs={{1,0},{2,1},{3,2},{4,3},{5,4},{6,5},{7,6},{8,7},{9,8},{10,9},{11,1... | collective-permute-start | bytes 98312 | tf_op jit(solution)/shard_map/ppermute | solution.py:38
  301.2 8.8 %collective-permute-start.48 = (f32[64,128]{1,0:T(8,128)S(1)}, f32[64,128]{1,0:T(8,128)S(1)}, u32[]{:S(2)}, u32[]{:S(2)}) collective-permute-start(f32[64,128]{1,0:T(8,128)S(1)} %fusion.65), channel_id=1, source_target_pairs={{1,0},{2,1},{3,2},{4,3},{5,4},{6,5},{7,6},{8,7},{9,8},{10,9},{11,1... | collective-permute-start | bytes 98312 | tf_op jit(solution)/shard_map/ppermute | solution.py:38
  316.0 8.8 %collective-permute-start.50 = (f32[64,128]{1,0:T(8,128)S(1)}, f32[64,128]{1,0:T(8,128)S(1)}, u32[]{:S(2)}, u32[]{:S(2)}) collective-permute-start(f32[64,128]{1,0:T(8,128)S(1)} %fusion.64), channel_id=1, source_target_pairs={{1,0},{2,1},{3,2},{4,3},{5,4},{6,5},{7,6},{8,7},{9,8},{10,9},{11,1... | collective-permute-start | bytes 98312 | tf_op jit(solution)/shard_map/ppermute | solution.py:38
  330.9 8.8 %collective-permute-start.52 = (f32[64,128]{1,0:T(8,128)S(1)}, f32[64,128]{1,0:T(8,128)S(1)}, u32[]{:S(2)}, u32[]{:S(2)}) collective-permute-start(f32[64,128]{1,0:T(8,128)S(1)} %fusion.63), channel_id=1, source_target_pairs={{1,0},{2,1},{3,2},{4,3},{5,4},{6,5},{7,6},{8,7},{9,8},{10,9},{11,1... | collective-permute-start | bytes 98312 | tf_op jit(solution)/shard_map/ppermute | solution.py:38
  345.7 8.8 %collective-permute-start.54 = (f32[64,128]{1,0:T(8,128)S(1)}, f32[64,128]{1,0:T(8,128)S(1)}, u32[]{:S(2)}, u32[]{:S(2)}) collective-permute-start(f32[64,128]{1,0:T(8,128)S(1)} %fusion.62), channel_id=1, source_target_pairs={{1,0},{2,1},{3,2},{4,3},{5,4},{6,5},{7,6},{8,7},{9,8},{10,9},{11,1... | collective-permute-start | bytes 98312 | tf_op jit(solution)/shard_map/ppermute | solution.py:38
  364.5 6.7 %collective-permute-start.59 = (f32[128,128]{1,0:T(8,128)S(1)}, f32[128,128]{1,0:T(8,128)S(1)}, u32[]{:S(2)}, u32[]{:S(2)}) collective-permute-start(f32[128,128]{1,0:T(8,128)S(1)} %get-tuple-element.220), channel_id=1, source_target_pairs={{0,7},{1,0},{2,1},{3,2},{4,3},{5,4},{6,5},{7,6},{8,15},{9,8},{10,9... | collective-permute-start | bytes 196616 | tf_op jit(solution)/shard_map/ppermute | solution.py:28
  366.4 6.0 %collective-permute-start.57 = (f32[128,128]{1,0:T(8,128)S(1)}, f32[128,128]{1,0:T(8,128)S(1)}, u32[]{:S(2)}, u32[]{:S(2)}) collective-permute-start(f32[128,128]{1,0:T(8,128)S(1)} %collective-permute-done.56), channel_id=1, source_target_pairs={{0,1},{1,2},{2,3},{3,4},{4,5},{5,6},{6,7},{7,0},{8,9},{9,10},{10,1... | collective-permute-start | bytes 196616 | tf_op jit(solution)/shard_map/ppermute | solution.py:25
  396.7 6.0 %collective-permute-start.65 = (f32[128,128]{1,0:T(8,128)S(1)}, f32[128,128]{1,0:T(8,128)S(1)}, u32[]{:S(2)}, u32[]{:S(2)}) collective-permute-start(f32[128,128]{1,0:T(8,128)S(1)} %collective-permute-done.64), channel_id=1, source_target_pairs={{0,1},{1,2},{2,3},{3,4},{4,5},{5,6},{6,7},{7,0},{8,9},{9,10},{10,1... | collective-permute-start | bytes 196616 | tf_op jit(solution)/shard_map/ppermute | solution.py:25
  401.3 6.8 %collective-permute-start.68 = (f32[128,128]{1,0:T(8,128)S(1)}, f32[128,128]{1,0:T(8,128)S(1)}, u32[]{:S(2)}, u32[]{:S(2)}) collective-permute-start(f32[128,128]{1,0:T(8,128)S(1)} %collective-permute-done.67), channel_id=1, source_target_pairs={{0,7},{1,0},{2,1},{3,2},{4,3},{5,4},{6,5},{7,6},{8,15},{9,8},{10,9... | collective-permute-start | bytes 196616 | tf_op jit(solution)/shard_map/ppermute | solution.py:28
  441.0 6.3 %collective-permute-start.78 = (f32[128,128]{1,0:T(8,128)S(1)}, f32[128,128]{1,0:T(8,128)S(1)}, u32[]{:S(2)}, u32[]{:S(2)}) collective-permute-start(f32[128,128]{1,0:T(8,128)S(1)} %collective-permute-done.77), channel_id=1, source_target_pairs={{0,1},{1,2},{2,3},{3,4},{4,5},{5,6},{6,7},{7,0},{8,9},{9,10},{10,1... | collective-permute-start | bytes 196616 | tf_op jit(solution)/shard_map/ppermute | solution.py:25
  445.5 6.8 %collective-permute-start.81 = (f32[128,128]{1,0:T(8,128)S(1)}, f32[128,128]{1,0:T(8,128)S(1)}, u32[]{:S(2)}, u32[]{:S(2)}) collective-permute-start(f32[128,128]{1,0:T(8,128)S(1)} %collective-permute-done.80), channel_id=1, source_target_pairs={{0,7},{1,0},{2,1},{3,2},{4,3},{5,4},{6,5},{7,6},{8,15},{9,8},{10,9... | collective-permute-start | bytes 196616 | tf_op jit(solution)/shard_map/ppermute | solution.py:28
  447.3 6.2 %collective-permute-start.79 = (f32[128,128]{1,0:T(8,128)S(1)}, f32[128,128]{1,0:T(8,128)S(1)}, u32[]{:S(2)}, u32[]{:S(2)}) collective-permute-start(f32[128,128]{1,0:T(8,128)S(1)} %collective-permute-done.78), channel_id=1, source_target_pairs={{0,1},{1,2},{2,3},{3,4},{4,5},{5,6},{6,7},{7,0},{8,9},{9,10},{10,1... | collective-permute-start | bytes 196616 | tf_op jit(solution)/shard_map/ppermute | solution.py:25
  476.6 6.0 %collective-permute-start.89 = (f32[128,128]{1,0:T(8,128)S(1)}, f32[128,128]{1,0:T(8,128)S(1)}, u32[]{:S(2)}, u32[]{:S(2)}) collective-permute-start(f32[128,128]{1,0:T(8,128)S(1)} %collective-permute-done.88), channel_id=1, source_target_pairs={{0,7},{1,0},{2,1},{3,2},{4,3},{5,4},{6,5},{7,6},{8,15},{9,8},{10,9... | collective-permute-start | bytes 196616 | tf_op jit(solution)/shard_map/ppermute | solution.py:28
  485.6 25.2 %collective-permute-start.90 = (f32[64,128]{1,0:T(8,128)S(1)}, f32[64,128]{1,0:T(8,128)S(1)}, u32[]{:S(2)}, u32[]{:S(2)}) collective-permute-start(f32[64,128]{1,0:T(8,128)S(1)} %fusion.75), channel_id=1, source_target_pairs={{0,1},{1,2},{2,3},{3,4},{4,5},{5,6},{6,7},{7,8},{8,9},{9,10},{10,1... | collective-permute-start | bytes 98312 | tf_op jit(solution)/shard_map/ppermute | solution.py:38
  508.8 8.8 %collective-permute-start.91 = (f32[64,128]{1,0:T(8,128)S(1)}, f32[64,128]{1,0:T(8,128)S(1)}, u32[]{:S(2)}, u32[]{:S(2)}) collective-permute-start(f32[64,128]{1,0:T(8,128)S(1)} %fusion.61), channel_id=1, source_target_pairs={{1,0},{2,1},{3,2},{4,3},{5,4},{6,5},{7,6},{8,7},{9,8},{10,9},{11,1... | collective-permute-start | bytes 98312 | tf_op jit(solution)/shard_map/ppermute | solution.py:38
  523.6 8.8 %collective-permute-start.93 = (f32[64,128]{1,0:T(8,128)S(1)}, f32[64,128]{1,0:T(8,128)S(1)}, u32[]{:S(2)}, u32[]{:S(2)}) collective-permute-start(f32[64,128]{1,0:T(8,128)S(1)} %fusion.60), channel_id=1, source_target_pairs={{1,0},{2,1},{3,2},{4,3},{5,4},{6,5},{7,6},{8,7},{9,8},{10,9},{11,1... | collective-permute-start | bytes 98312 | tf_op jit(solution)/shard_map/ppermute | solution.py:38
  538.5 8.8 %collective-permute-start.95 = (f32[64,128]{1,0:T(8,128)S(1)}, f32[64,128]{1,0:T(8,128)S(1)}, u32[]{:S(2)}, u32[]{:S(2)}) collective-permute-start(f32[64,128]{1,0:T(8,128)S(1)} %fusion.59), channel_id=1, source_target_pairs={{1,0},{2,1},{3,2},{4,3},{5,4},{6,5},{7,6},{8,7},{9,8},{10,9},{11,1... | collective-permute-start | bytes 98312 | tf_op jit(solution)/shard_map/ppermute | solution.py:38
  555.0 8.8 %collective-permute-start.97 = (f32[64,128]{1,0:T(8,128)S(1)}, f32[64,128]{1,0:T(8,128)S(1)}, u32[]{:S(2)}, u32[]{:S(2)}) collective-permute-start(f32[64,128]{1,0:T(8,128)S(1)} %fusion.58), channel_id=1, source_target_pairs={{1,0},{2,1},{3,2},{4,3},{5,4},{6,5},{7,6},{8,7},{9,8},{10,9},{11,1... | collective-permute-start | bytes 98312 | tf_op jit(solution)/shard_map/ppermute | solution.py:38
  (82 other events, 477.8 us)
